TPU v7x, 32 devices: a whole 2x2x4 slice. The times are simulated.
32 devices in a mesh: grp: 2 (over y), lat: 8 (over z, x), layer: 2 (over core).
Axes of the slice: x: 2, y: 2, z: 4, core: 2. Of those that a mesh axis runs over, the one named last changes fastest.
Arguments:
- resid: bfloat16 [2, 1024, 2048], P('layer', 'grp'), parts along dimension 1, may hold values from -6 to 6
- targets: bfloat16 [1024, 2, 2048], P(('grp', 'lat', 'layer')), parts along dimension 0, may hold values from -6 to 6
- encoder: bfloat16 [2, 16384, 2048], P('layer', 'lat'), may hold values from -0.125 to 0.125
- enc_bias: float32 [2, 16384], P('layer', 'lat'), may hold values from -4 to 4
- decoder: bfloat16 [2, 2, 16384, 2048], P('layer', None, 'lat'), may hold values from -0.09375 to 0.09375
- blocks: int32 [2, 8, 32], P('layer', 'grp'), parts along dimension 1, may hold values from 0 to 127, all different within a row
Outputs:
- grad_encoder: bfloat16 [4, 16384, 2048], P(('grp', 'layer'), 'lat'), parts along dimension 0
- grad_decoder: bfloat16 [4, 2, 16384, 2048], P(('grp', 'layer'), None, 'lat'), parts along dimension 0
- encoder_bias_gradient: float32 [4, 16384], P(('grp', 'layer'), 'lat'), parts along dimension 0
There are 2 independent parts, one for each index of `grp`. A program takes and returns all parts, laid end to end along the dimension named above; an argument that names none is the same for every part. Nothing has to cross between parts.
Inputs may be any that keep to these rules, and one draw needn't show every extreme that they name: Each row of a tile lists 32 different blocks; every block is listed somewhere.
All inputs are finite; a program needn't handle non-finite values.
Results may differ from a plain program's by a relative error of at most 0.006.
Values may be sent and summed in bfloat16 or wider, within the bound.
A program may use at most 192 MiB of HBM per device.

v0:
```python
import math

import jax
import jax.numpy as jnp
from jax import lax
from jax.sharding import PartitionSpec as P

BLOCK = 128
TILE = 128
TOKENS = 512


def per_device(resid, targets, encoder, enc_bias, decoder, blocks):
    lat_count = encoder.shape[1]
    latent_offset = lax.axis_index("lat") * lat_count
    lat_block = (latent_offset + jnp.arange(lat_count, dtype=jnp.int32)) // BLOCK
    hits = jnp.any(blocks[:, :, :, None] == lat_block[None, None, None, :], axis=2).astype(
        jnp.float32
    )
    gate = jnp.repeat(hits, TILE, axis=1)
    preactivation = jnp.einsum("tup,tcp->tuc", resid, encoder, preferred_element_type=jnp.float32)
    act = ((preactivation + enc_bias[:, None, :]) * gate).astype(jnp.bfloat16)
    scale = math.sqrt(TOKENS)
    summed = lax.psum_scatter(
        jnp.einsum("snl,stld->ntd", act, decoder, preferred_element_type=jnp.float32),
        ("lat", "layer"),
        scatter_dimension=0,
        tiled=True,
    )
    local_error_signal = ((summed - targets.astype(jnp.float32)) / scale).astype(jnp.bfloat16)
    error_signal = lax.all_gather(local_error_signal, ("lat", "layer"), axis=0, tiled=True)
    grad_decoder = jnp.einsum(
        "snl,ntd->stld", act, error_signal, preferred_element_type=jnp.float32
    ).astype(jnp.bfloat16)
    grad_act = jnp.einsum(
        "ntd,stld->snl", error_signal, decoder, preferred_element_type=jnp.float32
    )
    preactivation_gradient = grad_act * gate
    encoder_bias_gradient = jnp.sum(preactivation_gradient, axis=1)
    grad_encoder = jnp.einsum(
        "avx,avg->axg",
        preactivation_gradient.astype(jnp.bfloat16),
        resid,
        preferred_element_type=jnp.float32,
    ).astype(jnp.bfloat16)
    return (grad_encoder, grad_decoder, encoder_bias_gradient)


def solution(mesh):
    placed = (
        P("layer", "grp", None),
        P(("grp", "lat", "layer"), None, None),
        P("layer", "lat", None),
        P("layer", "lat"),
        P("layer", None, "lat", None),
        P("layer", "grp", None),
    )
    return jax.shard_map(
        per_device,
        mesh=mesh,
        in_specs=placed,
        out_specs=(
            P(("grp", "layer"), "lat", None),
            P(("grp", "layer"), None, "lat", None),
            P(("grp", "layer"), "lat"),
        ),
        check_vma=False,
    )
```

profile of v0, /device:TPU:24, one launch (start us, length us, event | category | flops | bytes accessed | tf_op | source)
XLA Modules:
  0.0 256.2 jit_solution(13876522610116495033)
XLA Ops:
  7.2 0.0 copy-start
  7.2 0.0 reduce-scatter.2.cloned.1.call-start
  7.2 1.0 compare_reduce_fusion
  8.3 0.5 copy-done
  8.8 8.1 %fusion.11 = bf16[512,2048,1]{1,0,2:T(8,128)(2,1)S(1)} fusion(bf16[1,2048,2048]{2,1,0:T(8,128)(2,1)} %param.8, bf16[1,512,2048]{2,1,0:T(8,128)(2,1)S(1)} %copy-done, f32[4,2048]{1,0:T(4,128)S(1)} %convert_element_type.34, f32[2048]{0:T(1024)} %bitcast.67), kind=kOutput, calls=%fused_computation.13 | convolution fusion | flops 4298113024 | bytes 12623872 | tf_op jit(solution)/shard_map/tup,tcp->tuc/dot_general | solution.py:21
  16.9 0.0 copy-start.2
  16.9 1.3 copy-done.2
  18.2 14.5 %fusion.2 = f32[512,2,2048]{2,0,1:T(8,128)} fusion(bf16[512,2048,1]{1,0,2:T(8,128)(2,1)S(1)} %fusion.11, bf16[1,2,2048,2048]{3,2,1,0:T(8,128)(2,1)} %param.10), kind=kOutput, calls=%fused_computation.2 | convolution fusion | flops 8589934592 | bytes 27262976 | tf_op jit(solution)/shard_map/snl,stld->ntd/dot_general | solution.py:25
  32.7 0.0 copy-start.1
  32.7 0.0 reduce-scatter.2.cloned.1.call-update
  32.7 0.2 all-gather.2.cloned.1.call-start
  33.0 104.4 %reduce-scatter.2.cloned.1.call-done = f32[32,2,2048]{2,0,1:T(8,128)} async-done(((f32[512,2,2048]{2,0,1:T(8,128)}), f32[32,2,2048]{2,0,1:T(8,128)}) %reduce-scatter.2.cloned.1.call-update) | async-done | bytes 524304 | tf_op jit(solution)/shard_map/reduce_scatter | solution.py:24
  137.4 0.0 copy-done.1
  137.4 1.9 multiply_convert_fusion
  139.3 0.0 all-gather.2.cloned.1.call-update
  139.3 50.9 %all-gather.2.cloned.1.call-done = bf16[512,2,2048]{2,0,1:T(8,128)(2,1)} async-done(((bf16[32,2,2048]{2,0,1:T(8,128)(2,1)}), bf16[512,2,2048]{2,0,1:T(8,128)(2,1)}) %all-gather.2.cloned.1.call-update) | async-done | bytes 4194320 | tf_op jit(solution)/shard_map/all_gather | solution.py:31
  190.2 15.0 %convert_bitcast_fusion = bf16[1,2,2048,2048]{2,3,1,0:T(8,128)(2,1)} fusion(bf16[512,2,2048]{2,0,1:T(8,128)(2,1)} %all-gather.2.cloned.1.call-done, bf16[512,2048,1]{1,0,2:T(8,128)(2,1)} %copy-done.2), kind=kOutput, calls=%fused_computation.4 | convolution fusion | flops 8598323200 | bytes 23068672 | tf_op jit(solution)/shard_map/snl,ntd->stld/dot_general | solution.py:32
  205.2 22.4 %copy.12 = bf16[1,2,2048,2048]{3,2,1,0:T(8,128)(2,1)} copy(bf16[1,2,2048,2048]{2,3,1,0:T(8,128)(2,1)} %convert_bitcast_fusion) | data formatting | bytes 33554432
  227.5 13.0 %fusion = f32[512,2048,1]{1,0,2:T(8,128)S(1)} fusion(bf16[512,2,2048]{2,0,1:T(8,128)(2,1)} %all-gather.2.cloned.1.call-done, bf16[1,2,2048,2048]{3,2,1,0:T(8,128)(2,1)} %param.10), kind=kOutput, calls=%fused_computation | convolution fusion | flops 8589934592 | bytes 25165824 | tf_op jit(solution)/shard_map/ntd,stld->snl/dot_general | solution.py:35
  240.5 0.5 broadcast_in_dim.10
  241.0 1.6 fusion.7
  242.6 6.8 %convert_bitcast_fusion.1 = bf16[1,2048,2048]{2,1,0:T(8,128)(2,1)} fusion(bf16[512,2048]{1,0:T(8,128)(2,1)S(1)} %get-tuple-element.10, bf16[1,512,2048]{2,1,0:T(8,128)(2,1)S(1)} %copy-done), kind=kOutput, calls=%fused_computation.7 | convolution fusion | flops 4299161600 | bytes 12582912 | tf_op jit(solution)/shard_map/avx,avg->axg/dot_general | solution.py:40
  (2 shorter events, 0.0 us)
Async XLA Ops:
  7.2 1.6 copy-start
  7.2 130.2 %reduce-scatter.2.cloned.1.call-start = ((), (), s32[]{:S(2)}) async-start(), calls=%async_computation.1 | async-start | bytes 8912896 | tf_op jit(solution)/shard_map/reduce_scatter | solution.py:24
  16.9 1.3 copy-start.2
  32.7 104.7 %copy-start.1 = (bf16[32,2,2048]{2,1,0:T(2,128)(2,1)S(1)}, bf16[32,2,2048]{2,1,0:T(2,128)(2,1)}, u32[]{:S(2)}) copy-start(bf16[32,2,2048]{2,1,0:T(2,128)(2,1)} %param.7) | copy-start | bytes 786436
  32.7 157.5 %all-gather.2.cloned.1.call-start = ((), (), s32[]{:S(2)}) async-start(), calls=%async_computation.2 | async-start | bytes 4456448 | tf_op jit(solution)/shard_map/all_gather | solution.py:31
Sparse Core Ops, SparseCore 0:
  32.9 104.4 reduce-scatter.1
  140.2 49.9 all-gather.1
where the time goes:
time: 260 us; the launch traced here: 256 us
  waiting for transfers between devices  155 us (60%)
  matrix products  57.3 us (22%)
  local copies, waits for them, and re-layouts  24.6 us (9%)
  between operations  14.1 us (5%)
  other arithmetic  4.56 us (2%)
    reduce_scatter x1, waiting for transfers between devices, per_device(): lax.psum_scatter(jnp.einsum('snl,stld->ntd', act, decoder, preferred_elem...  104 us
    all_gather x1, waiting for transfers between devices, per_device(): lax.all_gather(local_error_signal, ('lat', 'layer'), axis=0, tiled=True)  50.9 us
    unnamed x7, local copies, waits for them, and re-layouts  24.1 us
    dot_general x1, matrix products, per_device(): jnp.einsum('snl,ntd->stld', act, error_signal, preferred_element_type=jnp...  15 us
    dot_general x1, matrix products, per_device(): jnp.einsum('snl,stld->ntd', act, decoder, preferred_element_type=jnp.floa...  14.5 us
    dot_general x1, matrix products, per_device(): jnp.einsum('ntd,stld->snl', error_signal, decoder, preferred_element_type...  13 us
    dot_general x1, matrix products, per_device(): jnp.einsum('tup,tcp->tuc', resid, encoder, preferred_element_type=jnp.flo...  8.14 us
    dot_general x1, matrix products, per_device(): jnp.einsum('avx,avg->axg', preactivation_gradient.astype(jnp.bfloat16), r...  6.78 us
  transfers between devices with their start and end apart: 2, of which 2 were waited for; matrix products, arithmetic and copies ran while one was open for 0% of the time, Pallas kernels for 0%

commit v1 on v0

v1 whole, which is shorter than its diff:
```python
import functools
import math

import jax
import jax.numpy as jnp
from jax import lax
from jax.experimental import pallas as pl
from jax.experimental.pallas import tpu as pltpu
from jax.sharding import PartitionSpec as P

BLOCK = 128
TILE = 128
CHUNKS = 4
MIB = 1 << 20
MESH = pl.DeviceIdType.MESH


def dot_nt(a, b):
    return lax.dot_general(a, b, (((1,), (1,)), ((), ())), preferred_element_type=jnp.float32)


def dot_nn(a, b):
    return jnp.dot(a, b, preferred_element_type=jnp.float32)


def chunk_place(k, width, cc):
    per = width // cc
    return k // per, (k % per) * cc


def decode_kernel(hits, resid_ref, enc_ref, bias_ref, dec_ref, act_ref, recon_ref, acc_ref):
    b = pl.program_id(0)
    chunks, tokens, cc = recon_ref.shape
    width = dec_ref.shape[2]

    @pl.when(b == 0)
    def _():
        acc_ref[...] = jnp.zeros_like(acc_ref)

    for n in range(tokens // TILE):
        rows = slice(n * TILE, (n + 1) * TILE)
        hit = hits[n, b]

        @pl.when(hit > 0)
        def _(rows=rows):
            a = (dot_nt(resid_ref[rows], enc_ref[...]) + bias_ref[...]).astype(jnp.bfloat16)
            act_ref[0, rows] = a
            for k in range(chunks):
                t, col = chunk_place(k, width, cc)
                acc_ref[k, rows] += dot_nn(a, dec_ref[t, :, col : col + cc])

        @pl.when(hit == 0)
        def _(rows=rows):
            act_ref[0, rows] = jnp.zeros((TILE, BLOCK), jnp.bfloat16)

    @pl.when(b == pl.num_programs(0) - 1)
    def _():
        recon_ref[...] = acc_ref[...].astype(jnp.bfloat16)


def encode_decode(hits, resid, encoder, enc_bias, decoder, chunks):
    tokens, width = resid.shape
    latents = encoder.shape[0]
    targets = decoder.shape[0]
    nb = latents // BLOCK
    cc = targets * width // chunks
    return pl.pallas_call(
        decode_kernel,
        grid_spec=pltpu.PrefetchScalarGridSpec(
            num_scalar_prefetch=1,
            grid=(nb,),
            in_specs=[
                pl.BlockSpec((tokens, width), lambda b, h: (0, 0)),
                pl.BlockSpec((BLOCK, width), lambda b, h: (b, 0)),
                pl.BlockSpec((1, BLOCK), lambda b, h: (0, b)),
                pl.BlockSpec((targets, BLOCK, width), lambda b, h: (0, b, 0)),
            ],
            out_specs=[
                pl.BlockSpec((1, tokens, BLOCK), lambda b, h: (b, 0, 0)),
                pl.BlockSpec((chunks, tokens, cc), lambda b, h: (0, 0, 0)),
            ],
            scratch_shapes=[pltpu.VMEM((chunks, tokens, cc), jnp.float32)],
        ),
        out_shape=[
            jax.ShapeDtypeStruct((nb, tokens, BLOCK), jnp.bfloat16),
            jax.ShapeDtypeStruct((chunks, tokens, cc), jnp.bfloat16),
        ],
        compiler_params=pltpu.CompilerParams(vmem_limit_bytes=48 * MIB),
        name="encode_decode",
    )(hits, resid, encoder, enc_bias, decoder)


def grads_kernel(hits, act_ref, dec_ref, sig_ref, resid_ref, genc_ref, gdec_ref, bias_ref):
    b = pl.program_id(0)
    chunks, tokens, cc = sig_ref.shape
    width = dec_ref.shape[2]
    tiles = tokens // TILE
    flags = [hits[n, b] for n in range(tiles)]
    count = sum(flags)
    first = jnp.int32(tiles - 1)
    for n in reversed(range(tiles)):
        first = jnp.where(flags[n] > 0, n, first)
    last = jnp.int32(0)
    for n in range(tiles):
        last = jnp.where(flags[n] > 0, n, last)

    def work(places, masks):
        rows = [pl.ds(pl.multiple_of(n * TILE, TILE), TILE) for n in places]
        back = []
        total = jnp.zeros((1, BLOCK), jnp.float32)
        for r, mask in zip(rows, masks):
            ga = jnp.zeros((TILE, BLOCK), jnp.float32)
            for k in range(chunks):
                t, col = chunk_place(k, width, cc)
                ga = ga + dot_nt(sig_ref[k, r], dec_ref[t, :, col : col + cc])
            if mask is not None:
                ga = ga * mask.astype(jnp.float32)
            total = total + jnp.sum(ga, axis=0, keepdims=True)
            back.append(ga.T.astype(jnp.bfloat16))
        bias_ref[...] = total
        acts = [act_ref[0, r].astype(jnp.float32).T.astype(jnp.bfloat16) for r in rows]
        for k in range(chunks):
            t, col = chunk_place(k, width, cc)
            out = dot_nn(acts[0], sig_ref[k, rows[0]])
            for i in range(1, len(rows)):
                out = out + dot_nn(acts[i], sig_ref[k, rows[i]])
            gdec_ref[t, :, col : col + cc] = out.astype(jnp.bfloat16)
        step = 1024 if width % 1024 == 0 else width
        for col in range(0, width, step):
            out = dot_nn(back[0], resid_ref[rows[0], col : col + step])
            for i in range(1, len(rows)):
                out = out + dot_nn(back[i], resid_ref[rows[i], col : col + step])
            genc_ref[:, col : col + step] = out.astype(jnp.bfloat16)

    @pl.when(count == 0)
    def _():
        bias_ref[...] = jnp.zeros_like(bias_ref)
        gdec_ref[...] = jnp.zeros_like(gdec_ref)
        genc_ref[...] = jnp.zeros_like(genc_ref)

    @pl.when(count == 1)
    def _():
        work([first], [None])

    @pl.when(count == 2)
    def _():
        work([first, last], [None, None])

    @pl.when(count > 2)
    def _():
        work(list(range(tiles)), flags)


def grads(hits, act, decoder, signal, resid):
    tokens, width = resid.shape
    targets, latents = decoder.shape[:2]
    chunks, _, cc = signal.shape
    nb = latents // BLOCK
    return pl.pallas_call(
        grads_kernel,
        grid_spec=pltpu.PrefetchScalarGridSpec(
            num_scalar_prefetch=1,
            grid=(nb,),
            in_specs=[
                pl.BlockSpec((1, tokens, BLOCK), lambda b, h: (b, 0, 0)),
                pl.BlockSpec((targets, BLOCK, width), lambda b, h: (0, b, 0)),
                pl.BlockSpec((chunks, tokens, cc), lambda b, h: (0, 0, 0)),
                pl.BlockSpec((tokens, width), lambda b, h: (0, 0)),
            ],
            out_specs=[
                pl.BlockSpec((BLOCK, width), lambda b, h: (b, 0)),
                pl.BlockSpec((targets, BLOCK, width), lambda b, h: (0, b, 0)),
                pl.BlockSpec((1, BLOCK), lambda b, h: (0, b)),
            ],
        ),
        out_shape=[
            jax.ShapeDtypeStruct((latents, width), jnp.bfloat16),
            jax.ShapeDtypeStruct((targets, latents, width), jnp.bfloat16),
            jax.ShapeDtypeStruct((1, latents), jnp.float32),
        ],
        compiler_params=pltpu.CompilerParams(vmem_limit_bytes=48 * MIB),
        name="gradients",
    )(hits, act, decoder, signal, resid)


def exchange_kernel(
    scale, p_ref, tgt_ref, out_ref, r0, s1, r1, s2, r2,
    core_send, core_recv, x_send, x_recv, z_send, z_recv,
):
    chunks, zs, xs, cores, rows, cc = p_ref.shape
    lat = lax.axis_index("lat")
    c = lax.axis_index("layer")
    z, x = lat // xs, lax.rem(lat, xs)
    f32 = jnp.float32

    def dev(dz, dx, dc):
        zz, xx = lax.rem(z + dz, zs), lax.rem(x + dx, xs)
        return {"lat": zz * xs + xx, "layer": lax.rem(c + dc, cores)}

    peers = [dev(0, 0, d) for d in range(1, cores)]
    peers += [dev(0, d, 0) for d in range(1, xs)]
    peers += [dev(d, 0, 0) for d in range(1, zs)]
    barrier = pltpu.get_barrier_semaphore()
    for peer in peers:
        pl.semaphore_signal(barrier, inc=1, device_id=peer, device_id_type=MESH)
    pl.semaphore_wait(barrier, len(peers))

    started = []

    def copy(src, dst, send, recv, to):
        return pltpu.make_async_remote_copy(
            src_ref=src, dst_ref=dst, send_sem=send, recv_sem=recv, device_id=to, device_id_type=MESH
        )

    def go(*a):
        d = copy(*a)
        d.start()
        started.append(d)

    def core_rs(k, d):
        to = lax.rem(c + d, cores)
        return (p_ref.at[k, :, :, to], r0.at[k, d - 1], core_send.at[0, k, d - 1],
                core_recv.at[0, k, d - 1], dev(0, 0, d))

    def x_rs(k, d):
        return (s1.at[k, d - 1], r1.at[k, d - 1], x_send.at[0, k, d - 1], x_recv.at[0, k, d - 1],
                dev(0, d, 0))

    def z_rs(k, d):
        return (s2.at[k, d - 1], r2.at[k, d - 1], z_send.at[0, k, d - 1], z_recv.at[0, k, d - 1],
                dev(d, 0, 0))

    def z_ag(k, d, zz):
        at = out_ref.at[k, zz, x, c]
        return (at, at, z_send.at[1, k, d - 1], z_recv.at[1, k, d - 1], dev(d, 0, 0))

    def x_ag(k, d, xx):
        at = out_ref.at[k, :, xx, c]
        return (at, at, x_send.at[1, k, d - 1], x_recv.at[1, k, d - 1], dev(0, d, 0))

    def core_ag(k, d, c2):
        at = out_ref.at[k, :, :, c2]
        return (at, at, core_send.at[1, k, d - 1], core_recv.at[1, k, d - 1], dev(0, 0, d))

    def part(k, zz, xx):
        total = p_ref[k, zz, xx, c].astype(f32)
        for i in range(cores - 1):
            total = total + r0[k, i, zz, xx].astype(f32)
        return total

    def stage_a(k):
        for d in range(1, cores):
            go(*core_rs(k, d))

    def stage_b(k):
        for d in range(1, cores):
            copy(*core_rs(k, d)).wait_recv()
        for d in range(1, xs):
            xx = lax.rem(x + d, xs)
            for zz in range(zs):
                s1[k, d - 1, zz] = part(k, zz, xx).astype(jnp.bfloat16)
            go(*x_rs(k, d))

    def line(k, zz):
        total = part(k, zz, x)
        for i in range(xs - 1):
            total = total + r1[k, i, zz].astype(f32)
        return total

    def stage_c(k):
        for d in range(1, xs):
            copy(*x_rs(k, d)).wait_recv()
        for d in range(1, zs):
            s2[k, d - 1] = line(k, lax.rem(z + d, zs)).astype(jnp.bfloat16)
            go(*z_rs(k, d))

    def stage_d(k):
        total = line(k, z)
        for d in range(1, zs):
            copy(*z_rs(k, d)).wait_recv()
            total = total + r2[k, d - 1].astype(f32)
        out_ref[k, z, x, c] = ((total - tgt_ref[k].astype(f32)) / scale).astype(jnp.bfloat16)
        for d in range(1, zs):
            go(*z_ag(k, d, z))

    def stage_e(k):
        for d in range(1, zs):
            copy(*z_ag(k, d, lax.rem(z - d + zs, zs))).wait_recv()
        for d in range(1, xs):
            go(*x_ag(k, d, x))

    def stage_f(k):
        for d in range(1, xs):
            copy(*x_ag(k, d, lax.rem(x - d + xs, xs))).wait_recv()
        for d in range(1, cores):
            go(*core_ag(k, d, c))

    def stage_g(k):
        for d in range(1, cores):
            copy(*core_ag(k, d, lax.rem(c - d + cores, cores))).wait_recv()

    stages = (stage_b, stage_c, stage_d, stage_e, stage_f, stage_g)
    for k in range(chunks):
        stage_a(k)
    for s in range(chunks + len(stages) - 1):
        for i, stage in enumerate(stages):
            if 0 <= s - i < chunks:
                stage(s - i)
    for d in started:
        d.wait_send()


def exchange(recon, targets, zs, xs, cores, scale):
    chunks, tokens, cc = recon.shape
    rows = tokens // (zs * xs * cores)
    bf16 = jnp.bfloat16
    dma = pltpu.SemaphoreType.DMA
    out = pl.pallas_call(
        functools.partial(exchange_kernel, scale),
        out_shape=jax.ShapeDtypeStruct((chunks, zs, xs, cores, rows, cc), bf16),
        in_specs=[pl.BlockSpec(memory_space=pltpu.VMEM)] * 2,
        out_specs=pl.BlockSpec(memory_space=pltpu.VMEM),
        scratch_shapes=[
            pltpu.VMEM((chunks, cores - 1, zs, xs, rows, cc), bf16),
            pltpu.VMEM((chunks, xs - 1, zs, rows, cc), bf16),
            pltpu.VMEM((chunks, xs - 1, zs, rows, cc), bf16),
            pltpu.VMEM((chunks, zs - 1, rows, cc), bf16),
            pltpu.VMEM((chunks, zs - 1, rows, cc), bf16),
            dma((2, chunks, cores - 1)),
            dma((2, chunks, cores - 1)),
            dma((2, chunks, xs - 1)),
            dma((2, chunks, xs - 1)),
            dma((2, chunks, zs - 1)),
            dma((2, chunks, zs - 1)),
        ],
        compiler_params=pltpu.CompilerParams(
            collective_id=0, has_side_effects=True, vmem_limit_bytes=40 * MIB
        ),
        name="exchange",
    )(recon.reshape(chunks, zs, xs, cores, rows, cc), targets)
    return out.reshape(chunks, tokens, cc)


def per_device(lat_size, layer_size, resid, targets, encoder, enc_bias, decoder, blocks):
    lat_count = encoder.shape[1]
    width = resid.shape[2]
    tokens = resid.shape[1]
    outs = decoder.shape[1]
    nb = lat_count // BLOCK
    lat_block = lax.axis_index("lat") * nb + jnp.arange(nb, dtype=jnp.int32)
    hits = jnp.any(blocks[0][:, :, None] == lat_block[None, None, :], axis=1).astype(jnp.int32)
    scale = math.sqrt(tokens)
    act, recon = encode_decode(hits, resid[0], encoder[0], enc_bias, decoder[0], CHUNKS)
    rows = targets.shape[0]
    cc = outs * width // CHUNKS
    wanted = targets.reshape(rows, CHUNKS, cc).transpose(1, 0, 2)
    xs = max(1, round(lat_size ** (1 / 3)))
    if rows % 16 == 0 and layer_size > 1 and 1 < xs < lat_size and lat_size % xs == 0:
        signal = exchange(recon, wanted, lat_size // xs, xs, layer_size, scale)
    else:
        summed = lax.psum_scatter(
            recon.astype(jnp.float32), ("lat", "layer"), scatter_dimension=1, tiled=True
        )
        mine = ((summed - wanted.astype(jnp.float32)) / scale).astype(jnp.bfloat16)
        signal = lax.all_gather(mine, ("lat", "layer"), axis=1, tiled=True)
    genc, gdec, gbias = grads(hits, act, decoder[0], signal, resid[0])
    return genc[None], gdec[None], gbias


def solution(mesh):
    placed = (
        P("layer", "grp", None),
        P(("grp", "lat", "layer"), None, None),
        P("layer", "lat", None),
        P("layer", "lat"),
        P("layer", None, "lat", None),
        P("layer", "grp", None),
    )
    return jax.shard_map(
        functools.partial(per_device, mesh.shape["lat"], mesh.shape["layer"]),
        mesh=mesh,
        in_specs=placed,
        out_specs=(
            P(("grp", "layer"), "lat", None),
            P(("grp", "layer"), None, "lat", None),
            P(("grp", "layer"), "lat"),
        ),
        check_vma=False,
    )
```

time: 260 us -> 148 us (0.57); the launches traced: 256 us -> 149 us
  waiting for transfers between devices: 155 us -> 0 us
  Pallas kernels: 0 us -> 139 us
  matrix products: 57.3 us -> 0 us
  local copies, waits for them, and re-layouts: 24.6 us -> 7.65 us
  between operations: 14.1 us -> 0.69 us
  other arithmetic: 4.56 us -> 0.9 us
    pallas_call x0 -> x3, Pallas kernels: none -> 139 us  [the longest x1 68.2 us: exchange(): pl.pallas_call(functools.partial(exchange_kernel, scale), out_shape=jax.S...]
    reduce_scatter x1 -> x0, waiting for transfers between devices: 104 us -> none  [per_device(): lax.psum_scatter(jnp.einsum('snl,stld->ntd', act, decoder, preferred_elem...]
    dot_general x5 -> x0, matrix products: 57.3 us -> none  [the longest x1 15 us: per_device(): jnp.einsum('snl,ntd->stld', act, error_signal, preferred_element_type=jnp...]
    all_gather x1 -> x0, waiting for transfers between devices: 50.9 us -> none  [per_device(): lax.all_gather(local_error_signal, ('lat', 'layer'), axis=0, tiled=True)]
    unnamed x7 -> x10, local copies, waits for them, and re-layouts: 24.1 us -> 6.55 us
  transfers between devices with their start and end apart: 2 -> 0, of which waited for: 2 -> 0; matrix products, arithmetic and copies ran while one was open for 0% -> 0% of each run, Pallas kernels for 0% -> 0%
where the time goes in v1:
time: 148 us; the launch traced here: 149 us
  Pallas kernels  139 us (94%)
  local copies, waits for them, and re-layouts  7.65 us (5%)
    pallas_call x1, Pallas kernels, exchange(): pl.pallas_call(functools.partial(exchange_kernel, scale), out_shape=jax.S...  68.2 us
    pallas_call x1, Pallas kernels, grads(): pl.pallas_call(grads_kernel, grid_spec=pltpu.PrefetchScalarGridSpec(num_s...  36.5 us
    pallas_call x1, Pallas kernels, encode_decode(): pl.pallas_call(decode_kernel, grid_spec=pltpu.PrefetchScalarGridSpec(num_...  34.6 us
    unnamed x10, local copies, waits for them, and re-layouts  6.55 us

profile of v1, /device:TPU:24, one launch (start us, length us, event | category | flops | bytes accessed | tf_op | source)
XLA Modules:
  0.0 148.6 jit_solution(10865426623140036362)
XLA Ops:
  0.6 0.9 compare_reduce_fusion
  1.5 1.0 reshape.21
  2.6 0.1 copy.12
  2.7 0.0 copy-start.1
  2.7 1.6 %copy-done.1 = bf16[1,512,2048]{2,1,0:T(8,128)(2,1)S(1)} copy-done((bf16[1,512,2048]{2,1,0:T(8,128)(2,1)S(1)}, bf16[1,512,2048]{2,1,0:T(8,128)(2,1)}, u32[]{:S(2)}) %copy-start.1) | copy-done | bytes 2097176
  4.3 0.0 copy-start.4
  4.3 0.7 copy-done.4
  5.0 34.6 %encode_decode.1 = (bf16[16,512,128]{2,1,0:T(8,128)(2,1)S(1)}, bf16[4,512,1024]{2,1,0:T(8,128)(2,1)}) custom-call(s32[4,16]{1,0:T(4,128)S(1)} %convert_element_type.3.hits, bf16[512,2048]{1,0:T(8,128)(2,1)S(1)} %bitcast.12, bf16[2048,2048]{1,0:T(8,128)(2,1)} %bitcast.18, f32[1,2048]{1,0:T(1,128)S(1)} %copy-done.4, bf16[2,2048,2048]{2,1,0:T(8,128)(2,1)} %bitcast.16), custom_call_target="tpu_custom_call" | custom-call | tf_op jit(solution)/shard_map/encode_decode/pallas_call | solution.py:67
  39.6 0.0 copy-start.2
  39.6 0.0 copy-start.3
  39.6 2.3 %copy-done.3 = bf16[4,512,1024]{2,1,0:T(8,128)(2,1)S(1)} copy-done((bf16[4,512,1024]{2,1,0:T(8,128)(2,1)S(1)}, bf16[4,512,1024]{2,1,0:T(8,128)(2,1)}, u32[]{:S(2)}) %copy-start.3) | copy-done | bytes 4194328
  41.9 68.2 %exchange.1 = bf16[4,4,2,2,32,1024]{5,4,3,2,1,0:T(8,128)(2,1)S(1)} custom-call(bf16[4,4,2,2,32,1024]{5,4,3,2,1,0:T(8,128)(2,1)S(1)} %bitcast.14, bf16[4,32,1024]{2,1,0:T(8,128)(2,1)S(1)} %bitcast.15), custom_call_target="tpu_custom_call" | custom-call | tf_op jit(solution)/shard_map/exchange/pallas_call | solution.py:318
  110.1 0.0 copy-start
  110.1 1.9 %copy-done = bf16[4,4,2,2,32,1024]{5,4,3,2,1,0:T(8,128)(2,1)} copy-done((bf16[4,4,2,2,32,1024]{5,4,3,2,1,0:T(8,128)(2,1)}, bf16[4,4,2,2,32,1024]{5,4,3,2,1,0:T(8,128)(2,1)S(1)}, u32[]{:S(2)}) %copy-start) | copy-done | bytes 4194328
  112.1 0.0 copy-done.2
  112.1 36.5 %gradients.1 = (bf16[2048,2048]{1,0:T(8,128)(2,1)}, bf16[2,2048,2048]{2,1,0:T(8,128)(2,1)}, f32[1,2048]{1,0:T(1,128)}) custom-call(s32[4,16]{1,0:T(4,128)S(1)} %convert_element_type.3.hits, bf16[16,512,128]{2,1,0:T(8,128)(2,1)S(1)} %get-tuple-element.8.act_ref, bf16[2,2048,2048]{2,1,0:T(8,128)(2,1)} %bitcast.17, bf16[4,512,1024]{2,1,0:T(8,128)(2,1)} %bitcast.11, ...), custom_call_target="tpu_custom_call" | custom-call | tf_op jit(solution)/shard_map/gradients/pallas_call | solution.py:159
  (2 shorter events, 0.0 us)
Async XLA Ops:
  2.7 1.6 %copy-start.1 = (bf16[1,512,2048]{2,1,0:T(8,128)(2,1)S(1)}, bf16[1,512,2048]{2,1,0:T(8,128)(2,1)}, u32[]{:S(2)}) copy-start(bf16[1,512,2048]{2,1,0:T(8,128)(2,1)} %param.6) | copy-start | bytes 6291460
  4.3 0.7 copy-start.4
  39.6 72.5 %copy-start.2 = (bf16[1,512,2048]{2,1,0:T(8,128)(2,1)S(1)}, bf16[1,512,2048]{2,1,0:T(8,128)(2,1)}, u32[]{:S(2)}) copy-start(bf16[1,512,2048]{2,1,0:T(8,128)(2,1)} %param.6) | copy-start | bytes 6291460
  39.6 2.3 %copy-start.3 = (bf16[4,512,1024]{2,1,0:T(8,128)(2,1)S(1)}, bf16[4,512,1024]{2,1,0:T(8,128)(2,1)}, u32[]{:S(2)}) copy-start(bf16[4,512,1024]{2,1,0:T(8,128)(2,1)} %get-tuple-element.9) | copy-start | bytes 12582916
  110.1 1.9 %copy-start = (bf16[4,4,2,2,32,1024]{5,4,3,2,1,0:T(8,128)(2,1)}, bf16[4,4,2,2,32,1024]{5,4,3,2,1,0:T(8,128)(2,1)S(1)}, u32[]{:S(2)}) copy-start(bf16[4,4,2,2,32,1024]{5,4,3,2,1,0:T(8,128)(2,1)S(1)} %exchange.1) | copy-start | bytes 12582916

commit v2 on v1

v2 whole, which is shorter than its diff:
```python
import functools
import math

import jax
import jax.numpy as jnp
from jax import lax
from jax.experimental import pallas as pl
from jax.experimental.pallas import tpu as pltpu
from jax.sharding import PartitionSpec as P

BLOCK = 128
TILE = 128
CHUNKS = 8
MIB = 1 << 20
MESH = pl.DeviceIdType.MESH


def dot_nt(a, b):
    return lax.dot_general(a, b, (((1,), (1,)), ((), ())), preferred_element_type=jnp.float32)


def dot_nn(a, b):
    return jnp.dot(a, b, preferred_element_type=jnp.float32)


def chunk_place(k, width, cc):
    per = width // cc
    return k // per, (k % per) * cc


def encode_kernel(hits, resid_ref, enc_ref, bias_ref, act_ref):
    b = pl.program_id(0)
    tokens, size = act_ref.shape
    per = size // BLOCK
    pre = dot_nt(resid_ref[...], enc_ref[...]) + bias_ref[...]
    for n in range(tokens // TILE):
        for h in range(per):
            hit = hits[n, b * per + h].astype(jnp.float32)
            rows = slice(n * TILE, (n + 1) * TILE)
            cols = slice(h * BLOCK, (h + 1) * BLOCK)
            act_ref[rows, cols] = (pre[rows, cols] * hit).astype(jnp.bfloat16)


def encode(hits, resid, encoder, enc_bias):
    tokens, width = resid.shape
    latents = encoder.shape[0]
    size = min(2 * BLOCK, latents)
    return pl.pallas_call(
        encode_kernel,
        grid_spec=pltpu.PrefetchScalarGridSpec(
            num_scalar_prefetch=1,
            grid=(latents // size,),
            in_specs=[
                pl.BlockSpec((tokens, width), lambda b, h: (0, 0)),
                pl.BlockSpec((size, width), lambda b, h: (b, 0)),
                pl.BlockSpec((1, size), lambda b, h: (0, b)),
            ],
            out_specs=pl.BlockSpec((tokens, size), lambda b, h: (0, b)),
        ),
        out_shape=jax.ShapeDtypeStruct((tokens, latents), jnp.bfloat16),
        compiler_params=pltpu.CompilerParams(vmem_limit_bytes=32 * MIB),
        name="encode",
    )(hits, resid, encoder, enc_bias)


def grads_kernel(act_ref, ga_ref, sig_ref, resid_ref, genc_ref, gdec_ref):
    chunks, _, cc = sig_ref.shape
    width = resid_ref.shape[1]
    act = act_ref[...].astype(jnp.float32).T.astype(jnp.bfloat16)
    for k in range(chunks):
        t, col = chunk_place(k, width, cc)
        gdec_ref[t, :, col : col + cc] = dot_nn(act, sig_ref[k]).astype(jnp.bfloat16)
    back = ga_ref[...].astype(jnp.float32).T.astype(jnp.bfloat16)
    for col in range(0, width, cc):
        genc_ref[:, col : col + cc] = dot_nn(back, resid_ref[:, col : col + cc]).astype(jnp.bfloat16)


def grads(act, ga, signal, resid, targets):
    tokens, width = resid.shape
    latents = act.shape[1]
    chunks, _, cc = signal.shape
    size = min(2 * BLOCK, latents)
    return pl.pallas_call(
        grads_kernel,
        grid=(latents // size,),
        in_specs=[
            pl.BlockSpec((tokens, size), lambda b: (0, b)),
            pl.BlockSpec((tokens, size), lambda b: (0, b)),
            pl.BlockSpec((chunks, tokens, cc), lambda b: (0, 0, 0)),
            pl.BlockSpec((tokens, width), lambda b: (0, 0)),
        ],
        out_specs=[
            pl.BlockSpec((size, width), lambda b: (b, 0)),
            pl.BlockSpec((targets, size, width), lambda b: (0, b, 0)),
        ],
        out_shape=[
            jax.ShapeDtypeStruct((latents, width), jnp.bfloat16),
            jax.ShapeDtypeStruct((targets, latents, width), jnp.bfloat16),
        ],
        compiler_params=pltpu.CompilerParams(vmem_limit_bytes=48 * MIB),
        name="gradients",
    )(act, ga, signal, resid)


def exchange_kernel(
    scale, act_hbm, dec_hbm, tgt_ref, gate_ref, out_ref, ga_ref, bias_ref,
    p_ref, act_ref, dec_ref, acc_ref, r0, s1, r1, s2, r2,
    core_send, core_recv, x_send, x_recv, z_send, z_recv, act_sem, dec_sem,
):
    chunks, zs, xs, cores, rows, cc = p_ref.shape
    lat = lax.axis_index("lat")
    c = lax.axis_index("layer")
    z, x = lat // xs, lax.rem(lat, xs)
    f32 = jnp.float32

    def dev(dz, dx, dc):
        zz, xx = lax.rem(z + dz, zs), lax.rem(x + dx, xs)
        return {"lat": zz * xs + xx, "layer": lax.rem(c + dc, cores)}

    peers = [dev(0, 0, d) for d in range(1, cores)]
    peers += [dev(0, d, 0) for d in range(1, xs)]
    peers += [dev(d, 0, 0) for d in range(1, zs)]
    tokens, latents = act_ref.shape
    width = dec_hbm.shape[2]
    per = width // cc

    def load_dec(k):
        cols = pl.ds(pl.multiple_of(lax.rem(k, per) * cc, cc), cc)
        return pltpu.make_async_copy(dec_hbm.at[k // per, :, cols], dec_ref.at[k], dec_sem.at[k])

    load_act = pltpu.make_async_copy(act_hbm, act_ref, act_sem)
    load_act.start()
    for k in range(chunks):
        load_dec(jnp.int32(k)).start()
    barrier = pltpu.get_barrier_semaphore()
    for peer in peers:
        pl.semaphore_signal(barrier, inc=1, device_id=peer, device_id_type=MESH)
    pl.semaphore_wait(barrier, len(peers))

    def copy(src, dst, send, recv, to):
        return pltpu.make_async_remote_copy(
            src_ref=src, dst_ref=dst, send_sem=send, recv_sem=recv, device_id=to, device_id_type=MESH
        )

    def go(*a):
        copy(*a).start()

    def core_rs(k, d):
        to = lax.rem(c + d, cores)
        return (p_ref.at[k, :, :, to], r0.at[k, d - 1], core_send.at[0, k, d - 1],
                core_recv.at[0, k, d - 1], dev(0, 0, d))

    def x_rs(k, d):
        return (s1.at[k, d - 1], r1.at[k, d - 1], x_send.at[0, k, d - 1], x_recv.at[0, k, d - 1],
                dev(0, d, 0))

    def z_rs(k, d):
        return (s2.at[k, d - 1], r2.at[k, d - 1], z_send.at[0, k, d - 1], z_recv.at[0, k, d - 1],
                dev(d, 0, 0))

    def z_ag(k, d, zz):
        at = out_ref.at[k, zz, x, c]
        return (at, at, z_send.at[1, k, d - 1], z_recv.at[1, k, d - 1], dev(d, 0, 0))

    def x_ag(k, d, xx):
        at = out_ref.at[k, :, xx, c]
        return (at, at, x_send.at[1, k, d - 1], x_recv.at[1, k, d - 1], dev(0, d, 0))

    def core_ag(k, d, c2):
        at = out_ref.at[k, :, :, c2]
        return (at, at, core_send.at[1, k, d - 1], core_recv.at[1, k, d - 1], dev(0, 0, d))

    def part(k, zz, xx):
        total = p_ref[k, zz, xx, c].astype(f32)
        for i in range(cores - 1):
            total = total + r0[k, i, zz, xx].astype(f32)
        return total

    def stage_a(k):
        load_dec(k).wait()
        part_sum = dot_nn(act_ref[...], dec_ref[k]).astype(jnp.bfloat16)
        p_ref[k] = part_sum.reshape(zs, xs, cores, rows, cc)
        for d in range(1, cores):
            go(*core_rs(k, d))

    def stage_b(k):
        for d in range(1, cores):
            copy(*core_rs(k, d)).wait_recv()
        for d in range(1, xs):
            xx = lax.rem(x + d, xs)
            for zz in range(zs):
                s1[k, d - 1, zz] = part(k, zz, xx).astype(jnp.bfloat16)
            go(*x_rs(k, d))

    def line(k, zz):
        total = part(k, zz, x)
        for i in range(xs - 1):
            total = total + r1[k, i, zz].astype(f32)
        return total

    def stage_c(k):
        for d in range(1, xs):
            copy(*x_rs(k, d)).wait_recv()
        for d in range(1, zs):
            s2[k, d - 1] = line(k, lax.rem(z + d, zs)).astype(jnp.bfloat16)
            go(*z_rs(k, d))

    def stage_d(k):
        total = line(k, z)
        for d in range(1, zs):
            copy(*z_rs(k, d)).wait_recv()
            total = total + r2[k, d - 1].astype(f32)
        out_ref[k, z, x, c] = ((total - tgt_ref[k].astype(f32)) / scale).astype(jnp.bfloat16)
        for d in range(1, zs):
            go(*z_ag(k, d, z))

    def stage_e(k):
        for d in range(1, zs):
            copy(*z_ag(k, d, lax.rem(z - d + zs, zs))).wait_recv()
        for d in range(1, xs):
            go(*x_ag(k, d, x))

    def stage_f(k):
        for d in range(1, xs):
            copy(*x_ag(k, d, lax.rem(x - d + xs, xs))).wait_recv()
        for d in range(1, cores):
            go(*core_ag(k, d, c))

    def stage_g(k):
        for d in range(1, cores):
            copy(*core_ag(k, d, lax.rem(c - d + cores, cores))).wait_recv()
        sig = out_ref[k].reshape(tokens, cc)

        @pl.loop(0, latents // step)
        def _(i):
            cols = pl.ds(pl.multiple_of(i * step, step), step)
            acc_ref[:, cols] += dot_nt(sig, dec_ref[k, cols])

    step = min(512, latents)
    acc_ref[...] = jnp.zeros_like(acc_ref)
    load_act.wait()
    stages = (stage_a, stage_b, stage_c, stage_d, stage_e, stage_f, stage_g)

    @pl.loop(0, chunks + len(stages) - 1)
    def _(s):
        for i, stage in enumerate(stages):
            k = s - i

            @pl.when((k >= 0) & (k < chunks))
            def _(k=k, stage=stage):
                stage(k)

    for n in range(tokens // TILE):
        at = slice(n * TILE, (n + 1) * TILE)
        back = acc_ref[at] * gate_ref[n]
        total = jnp.sum(back, axis=0, keepdims=True)
        bias_ref[...] = total if n == 0 else bias_ref[...] + total
        ga_ref[at] = back.astype(jnp.bfloat16)

    @pl.loop(0, chunks)
    def _(k):
        for d in range(1, cores):
            copy(*core_rs(k, d)).wait_send()
            copy(*core_ag(k, d, c)).wait_send()
        for d in range(1, xs):
            copy(*x_rs(k, d)).wait_send()
            copy(*x_ag(k, d, x)).wait_send()
        for d in range(1, zs):
            copy(*z_rs(k, d)).wait_send()
            copy(*z_ag(k, d, z)).wait_send()


def exchange(act, decoder, targets, gate, chunks, zs, xs, cores, scale):
    tokens, latents = act.shape
    outs, _, width = decoder.shape
    cc = outs * width // chunks
    rows = tokens // (zs * xs * cores)
    bf16 = jnp.bfloat16
    dma = pltpu.SemaphoreType.DMA
    vmem = pl.BlockSpec(memory_space=pltpu.VMEM)
    hbm = pl.BlockSpec(memory_space=pl.ANY)
    signal, ga, bias = pl.pallas_call(
        functools.partial(exchange_kernel, scale),
        out_shape=[
            jax.ShapeDtypeStruct((chunks, zs, xs, cores, rows, cc), bf16),
            jax.ShapeDtypeStruct((tokens, latents), bf16),
            jax.ShapeDtypeStruct((1, latents), jnp.float32),
        ],
        in_specs=[hbm, hbm, vmem, vmem],
        out_specs=[vmem, vmem, vmem],
        scratch_shapes=[
            pltpu.VMEM((chunks, zs, xs, cores, rows, cc), bf16),
            pltpu.VMEM((tokens, latents), bf16),
            pltpu.VMEM((chunks, latents, cc), bf16),
            pltpu.VMEM((tokens, latents), jnp.float32),
            pltpu.VMEM((chunks, cores - 1, zs, xs, rows, cc), bf16),
            pltpu.VMEM((chunks, xs - 1, zs, rows, cc), bf16),
            pltpu.VMEM((chunks, xs - 1, zs, rows, cc), bf16),
            pltpu.VMEM((chunks, zs - 1, rows, cc), bf16),
            pltpu.VMEM((chunks, zs - 1, rows, cc), bf16),
            dma((2, chunks, cores - 1)),
            dma((2, chunks, cores - 1)),
            dma((2, chunks, xs - 1)),
            dma((2, chunks, xs - 1)),
            dma((2, chunks, zs - 1)),
            dma((2, chunks, zs - 1)),
            dma,
            dma((chunks,)),
        ],
        compiler_params=pltpu.CompilerParams(
            collective_id=0, has_side_effects=True, vmem_limit_bytes=56 * MIB
        ),
        name="exchange",
    )(act, decoder, targets, gate)
    return signal.reshape(chunks, tokens, cc), ga, bias


def per_device(lat_size, layer_size, resid, targets, encoder, enc_bias, decoder, blocks):
    lat_count = encoder.shape[1]
    width = resid.shape[2]
    tokens = resid.shape[1]
    outs = decoder.shape[1]
    nb = lat_count // BLOCK
    lat_block = lax.axis_index("lat") * nb + jnp.arange(nb, dtype=jnp.int32)
    hits = jnp.any(blocks[0][:, :, None] == lat_block[None, None, :], axis=1).astype(jnp.int32)
    scale = math.sqrt(tokens)
    gate = jnp.repeat(hits, BLOCK, axis=1).astype(jnp.float32)[:, None, :]
    act = encode(hits, resid[0], encoder[0], enc_bias)
    rows = targets.shape[0]
    cc = outs * width // CHUNKS
    wanted = targets.reshape(rows, CHUNKS, cc).transpose(1, 0, 2)
    xs = max(1, round(lat_size ** (1 / 3)))
    if rows % 16 == 0 and layer_size > 1 and 1 < xs < lat_size and lat_size % xs == 0:
        signal, ga, gbias = exchange(
            act, decoder[0], wanted, gate, CHUNKS, lat_size // xs, xs, layer_size, scale
        )
    else:
        f32 = jnp.float32
        by_chunk = decoder[0].reshape(outs, lat_count, CHUNKS // outs, cc)
        by_chunk = by_chunk.transpose(0, 2, 1, 3).reshape(CHUNKS, lat_count, cc)
        recon = jnp.einsum("nl,kld->knd", act, by_chunk, preferred_element_type=f32)
        summed = lax.psum_scatter(recon, ("lat", "layer"), scatter_dimension=1, tiled=True)
        mine = ((summed - wanted.astype(f32)) / scale).astype(jnp.bfloat16)
        signal = lax.all_gather(mine, ("lat", "layer"), axis=1, tiled=True)
        back = jnp.einsum("knd,kld->nl", signal, by_chunk, preferred_element_type=f32)
        back = back * jnp.repeat(gate[:, 0], TILE, axis=0)
        gbias = jnp.sum(back, axis=0, keepdims=True)
        ga = back.astype(jnp.bfloat16)
    genc, gdec = grads(act, ga, signal, resid[0], outs)
    return genc[None], gdec[None], gbias


def solution(mesh):
    placed = (
        P("layer", "grp", None),
        P(("grp", "lat", "layer"), None, None),
        P("layer", "lat", None),
        P("layer", "lat"),
        P("layer", None, "lat", None),
        P("layer", "grp", None),
    )
    return jax.shard_map(
        functools.partial(per_device, mesh.shape["lat"], mesh.shape["layer"]),
        mesh=mesh,
        in_specs=placed,
        out_specs=(
            P(("grp", "layer"), "lat", None),
            P(("grp", "layer"), None, "lat", None),
            P(("grp", "layer"), "lat"),
        ),
        check_vma=False,
    )
```

time: 148 us -> 122 us (0.82); the launches traced: 149 us -> 121 us
  Pallas kernels: 139 us -> 106 us
  local copies, waits for them, and re-layouts: 7.65 us -> 13.2 us
    pallas_call x3, Pallas kernels: 139 us -> 106 us  [the longest x1 79.1 us: exchange(): pl.pallas_call(functools.partial(exchange_kernel, scale), out_shape=[jax....]
    unnamed x10 -> x15, local copies, waits for them, and re-layouts: 6.55 us -> 10.8 us
where the time goes in v2:
time: 122 us; the launch traced here: 121 us
  Pallas kernels  106 us (87%)
  local copies, waits for them, and re-layouts  13.2 us (11%)
    pallas_call x1, Pallas kernels, exchange(): pl.pallas_call(functools.partial(exchange_kernel, scale), out_shape=[jax....  79.1 us
    pallas_call x1, Pallas kernels, grads(): pl.pallas_call(grads_kernel, grid=(latents // size,), in_specs=[pl.BlockS...  20 us
    unnamed x15, local copies, waits for them, and re-layouts  10.8 us
    pallas_call x1, Pallas kernels, encode(): pl.pallas_call(encode_kernel, grid_spec=pltpu.PrefetchScalarGridSpec(num_...  6.79 us

profile of v2, /device:TPU:24, one launch (start us, length us, event | category | flops | bytes accessed | tf_op | source)
XLA Modules:
  0.0 120.8 jit_solution(15357871092535056240)
XLA Ops:
  0.6 0.9 compare_reduce_fusion
  1.6 0.7 broadcast_in_dim.11
  2.2 1.0 reshape.29
  3.3 0.8 copy.12
  4.0 0.0 copy-start.2
  4.0 3.4 %copy-done.2 = bf16[1,2048,2048]{2,1,0:T(8,128)(2,1)S(1)} copy-done((bf16[1,2048,2048]{2,1,0:T(8,128)(2,1)S(1)}, bf16[1,2048,2048]{2,1,0:T(8,128)(2,1)}, u32[]{:S(2)}) %copy-start.2) | copy-done | bytes 8388632
  7.4 0.0 copy-start.3
  7.4 1.6 %copy-done.3 = bf16[1,512,2048]{2,1,0:T(8,128)(2,1)S(1)} copy-done((bf16[1,512,2048]{2,1,0:T(8,128)(2,1)S(1)}, bf16[1,512,2048]{2,1,0:T(8,128)(2,1)}, u32[]{:S(2)}) %copy-start.3) | copy-done | bytes 2097176
  9.0 0.0 copy-start.5
  9.0 0.7 copy-done.5
  9.7 6.8 %encode.1.act_hbm.act_ref = bf16[512,2048]{1,0:T(8,128)(2,1)S(1)} custom-call(s32[4,16]{1,0:T(4,128)S(1)} %get-tuple-element.14.hits, bf16[512,2048]{1,0:T(8,128)(2,1)S(1)} %bitcast.13, bf16[2048,2048]{1,0:T(8,128)(2,1)S(1)} %bitcast.11, f32[1,2048]{1,0:T(1,128)S(1)} %copy-done.5), custom_call_target="tpu_custom_call" | custom-call | tf_op jit(solution)/shard_map/encode/pallas_call | solution.py:48
  16.5 0.0 copy-start
  16.5 1.3 %copy-done = bf16[512,2048]{1,0:T(8,128)(2,1)} copy-done((bf16[512,2048]{1,0:T(8,128)(2,1)}, bf16[512,2048]{1,0:T(8,128)(2,1)S(1)}, u32[]{:S(2)}) %copy-start) | copy-done | bytes 2097176
  17.8 79.1 %exchange.1 = (bf16[8,4,2,2,32,512]{5,4,3,2,1,0:T(8,128)(2,1)}, bf16[512,2048]{1,0:T(8,128)(2,1)}, f32[1,2048]{1,0:T(1,128)}) custom-call(bf16[512,2048]{1,0:T(8,128)(2,1)} %copy-done, bf16[2,2048,2048]{2,1,0:T(8,128)(2,1)} %bitcast.14, bf16[8,32,512]{2,1,0:T(8,128)(2,1)} %bitcast.16, f32[4,1,2048]{2,1,0:T(1,128)} %bitcast.17), custom_call_target="tpu_custom_call" | custom-call | tf_op jit(solution)/shard_map/exchange/pallas_call | solution.py:282
  96.9 0.0 copy-start.1
  97.0 1.6 %copy-done.1 = bf16[512,2048]{1,0:T(8,128)(2,1)S(1)} copy-done((bf16[512,2048]{1,0:T(8,128)(2,1)S(1)}, bf16[512,2048]{1,0:T(8,128)(2,1)}, u32[]{:S(2)}) %copy-start.1) | copy-done | bytes 2097176
  98.5 0.0 copy-start.4
  98.5 1.6 %copy-done.4 = bf16[512,2048]{1,0:T(8,128)(2,1)S(1)} copy-done((bf16[512,2048]{1,0:T(8,128)(2,1)S(1)}, bf16[512,2048]{1,0:T(8,128)(2,1)}, u32[]{:S(2)}) %copy-start.4) | copy-done | bytes 2097176
  100.1 0.0 copy-start.6
  100.1 20.0 %gradients.1 = (bf16[2048,2048]{1,0:T(8,128)(2,1)}, bf16[2,2048,2048]{2,1,0:T(8,128)(2,1)}) custom-call(bf16[512,2048]{1,0:T(8,128)(2,1)S(1)} %copy-done.1, bf16[512,2048]{1,0:T(8,128)(2,1)S(1)} %copy-done.4, bf16[8,512,512]{2,1,0:T(8,128)(2,1)} %bitcast.15, bf16[512,2048]{1,0:T(8,128)(2,1)} %bitcast.12), custom_call_target="tpu_custom_call" | custom-call | tf_op jit(solution)/shard_map/gradients/pallas_call | solution.py:83
  120.2 0.0 copy-done.6
  120.2 0.6 copy.14
  (2 shorter events, 0.0 us)
Async XLA Ops:
  4.0 3.4 %copy-start.2 = (bf16[1,2048,2048]{2,1,0:T(8,128)(2,1)S(1)}, bf16[1,2048,2048]{2,1,0:T(8,128)(2,1)}, u32[]{:S(2)}) copy-start(bf16[1,2048,2048]{2,1,0:T(8,128)(2,1)} %param.8) | copy-start | bytes 25165828
  7.4 1.6 %copy-start.3 = (bf16[1,512,2048]{2,1,0:T(8,128)(2,1)S(1)}, bf16[1,512,2048]{2,1,0:T(8,128)(2,1)}, u32[]{:S(2)}) copy-start(bf16[1,512,2048]{2,1,0:T(8,128)(2,1)} %param.6) | copy-start | bytes 6291460
  9.0 0.7 copy-start.5
  16.5 1.3 %copy-start = (bf16[512,2048]{1,0:T(8,128)(2,1)}, bf16[512,2048]{1,0:T(8,128)(2,1)S(1)}, u32[]{:S(2)}) copy-start(bf16[512,2048]{1,0:T(8,128)(2,1)S(1)} %encode.1.act_hbm.act_ref) | copy-start | bytes 6291460
  96.9 1.6 %copy-start.1 = (bf16[512,2048]{1,0:T(8,128)(2,1)S(1)}, bf16[512,2048]{1,0:T(8,128)(2,1)}, u32[]{:S(2)}) copy-start(bf16[512,2048]{1,0:T(8,128)(2,1)} %copy-done) | copy-start | bytes 6291460
  98.5 1.6 %copy-start.4 = (bf16[512,2048]{1,0:T(8,128)(2,1)S(1)}, bf16[512,2048]{1,0:T(8,128)(2,1)}, u32[]{:S(2)}) copy-start(bf16[512,2048]{1,0:T(8,128)(2,1)} %get-tuple-element.8.ga_ref) | copy-start | bytes 6291460
  100.1 20.1 %copy-start.6 = (f32[1,2048]{1,0:T(1,128)S(1)}, f32[1,2048]{1,0:T(1,128)}, u32[]{:S(2)}) copy-start(f32[1,2048]{1,0:T(1,128)} %get-tuple-element.20) | copy-start | bytes 24580

commit v3 on v2

--- a/solution.py
+++ b/solution.py
@@ -58,7 +58,7 @@
             out_specs=pl.BlockSpec((tokens, size), lambda b, h: (0, b)),
         ),
         out_shape=jax.ShapeDtypeStruct((tokens, latents), jnp.bfloat16),
-        compiler_params=pltpu.CompilerParams(vmem_limit_bytes=32 * MIB),
+        compiler_params=pltpu.CompilerParams(vmem_limit_bytes=60 * MIB),
         name="encode",
     )(hits, resid, encoder, enc_bias)
 
@@ -97,7 +97,7 @@
             jax.ShapeDtypeStruct((latents, width), jnp.bfloat16),
             jax.ShapeDtypeStruct((targets, latents, width), jnp.bfloat16),
         ],
-        compiler_params=pltpu.CompilerParams(vmem_limit_bytes=48 * MIB),
+        compiler_params=pltpu.CompilerParams(vmem_limit_bytes=60 * MIB),
         name="gradients",
     )(act, ga, signal, resid)
 
@@ -308,7 +308,7 @@
             dma((chunks,)),
         ],
         compiler_params=pltpu.CompilerParams(
-            collective_id=0, has_side_effects=True, vmem_limit_bytes=56 * MIB
+            collective_id=0, has_side_effects=True, vmem_limit_bytes=60 * MIB
         ),
         name="exchange",
     )(act, decoder, targets, gate)

time: 122 us -> 117 us (0.959)
  local copies, waits for them, and re-layouts: 13.2 us -> 3.09 us
  Pallas kernels: 106 us -> 110 us
    unnamed x15 -> x3, local copies, waits for them, and re-layouts: 10.8 us -> 0.6 us
    pallas_call x1, Pallas kernels: 6.79 us -> 11.3 us  [encode(): pl.pallas_call(encode_kernel, grid_spec=pltpu.PrefetchScalarGridSpec(num_...]
where the time goes in v3:
time: 117 us; the launch traced here: 115 us
  Pallas kernels  110 us (94%)
  local copies, waits for them, and re-layouts  3.09 us (3%)
  other arithmetic  1.49 us (1%)
    pallas_call x1, Pallas kernels, exchange(): pl.pallas_call(functools.partial(exchange_kernel, scale), out_shape=[jax....  79.1 us
    pallas_call x1, Pallas kernels, grads(): pl.pallas_call(grads_kernel, grid=(latents // size,), in_specs=[pl.BlockS...  19.8 us
    pallas_call x1, Pallas kernels, encode(): pl.pallas_call(encode_kernel, grid_spec=pltpu.PrefetchScalarGridSpec(num_...  11.3 us

profile of v3, /device:TPU:24, one launch (start us, length us, event | category | flops | bytes accessed | tf_op | source)
XLA Modules:
  0.0 115.5 jit_solution(7720420019914931598)
XLA Ops:
  0.6 0.9 compare_reduce_fusion
  1.5 0.6 convert_convert_fusion
  2.1 0.7 broadcast_in_dim.11
  2.8 1.0 reshape.29
  3.8 0.8 copy.12
  4.6 11.3 %encode.1.act_hbm.act_ref = bf16[512,2048]{1,0:T(8,128)(2,1)} custom-call(s32[4,16]{1,0:T(4,128)} %get-tuple-element.14.hits, bf16[512,2048]{1,0:T(8,128)(2,1)} %bitcast.13, bf16[2048,2048]{1,0:T(8,128)(2,1)} %bitcast.12, f32[1,2048]{1,0:T(1,128)} %bias_ref.1), custom_call_target="tpu_custom_call" | custom-call | tf_op jit(solution)/shard_map/encode/pallas_call | solution.py:48
  16.0 79.1 %exchange.1 = (bf16[8,4,2,2,32,512]{5,4,3,2,1,0:T(8,128)(2,1)}, bf16[512,2048]{1,0:T(8,128)(2,1)}, f32[1,2048]{1,0:T(1,128)}) custom-call(bf16[512,2048]{1,0:T(8,128)(2,1)} %encode.1.act_hbm.act_ref, bf16[2,2048,2048]{2,1,0:T(8,128)(2,1)} %bitcast.11, bf16[8,32,512]{2,1,0:T(8,128)(2,1)} %bitcast.16, f32[4,1,2048]{2,1,0:T(1,128)} %bitcast.17), custom_call_target="tpu_custom_call" | custom-call | tf_op jit(solution)/shard_map/exchange/pallas_call | solution.py:282
  95.0 0.0 copy-start
  95.0 19.8 %gradients.1 = (bf16[2048,2048]{1,0:T(8,128)(2,1)}, bf16[2,2048,2048]{2,1,0:T(8,128)(2,1)}) custom-call(bf16[512,2048]{1,0:T(8,128)(2,1)} %encode.1.act_hbm.act_ref, bf16[512,2048]{1,0:T(8,128)(2,1)} %get-tuple-element.8.ga_ref, bf16[8,512,512]{2,1,0:T(8,128)(2,1)} %bitcast.15, bf16[512,2048]{1,0:T(8,128)(2,1)} %bitcast.14), custom_call_target="tpu_custom_call" | custom-call | tf_op jit(solution)/shard_map/gradients/pallas_call | solution.py:83
  114.9 0.0 copy-done
  114.9 0.6 copy.14
  (1 shorter events, 0.0 us)
Async XLA Ops:
  95.0 19.8 %copy-start = (f32[1,2048]{1,0:T(1,128)S(1)}, f32[1,2048]{1,0:T(1,128)}, u32[]{:S(2)}) copy-start(f32[1,2048]{1,0:T(1,128)} %get-tuple-element.20) | copy-start | bytes 24580
